TPU v7x, 512 devices: a whole 4x4x16 slice. The times are simulated.
512 devices in a mesh: mem: 16 (over x, z_lo), tile: 32 (over y, z_hi, core).
Axes of the slice: x: 4, y: 4, z: 16 (z_hi: 4, z_lo: 4; z = z_hi * 4 + z_lo), core: 2. Of those that a mesh axis runs over, the one named last changes fastest.
Arguments:
- controls: float32 [128, 512, 1792], P('mem', 'tile'), may hold values from -6 to 6
- perturbations: bfloat16 [128, 4, 512, 1792], P('mem', None, 'tile'), may hold values from -1.5 to 1.5
- jacobian: float32 [4, 512, 1792], P(None, 'tile'), may hold values from -3 to 3
- obs_weight: float32 [512, 1792], P('tile'), may hold values from 0.5 to 4
- radar_mask: int32 [512, 1792], P('tile'), may hold values 0 or 1
- row_faces: float32 [512, 1792], P('tile'), may hold values from 0.12 to 0.25
- col_faces: float32 [512, 1792], P('tile'), may hold values from 0.12 to 0.25
Outputs:
- gradient: float32 [128, 512, 1792], P('mem', 'tile')
All inputs are finite; a program needn't handle non-finite values. No bound on the sum of `radar_mask` on one device may be relied on, other than what follows from the above.
Results may differ from a plain program's by a relative error of at most 0.0003.
Values sent between devices are 32-bit elements; how exact they have to be, the bound alone decides.
A program may use at most 64 MiB of HBM per device.

v0:
```python
import jax
import jax.numpy as jnp
from jax import lax
from jax.sharding import PartitionSpec as P

STEPS = 4


def padded(cells, sides, width):
    for axis, dim in sides:
        count = lax.axis_size(axis)
        ends = count - 1
        head = lax.slice_in_dim(cells, 0, width, axis=dim)
        tail = lax.slice_in_dim(cells, cells.shape[dim] - width, cells.shape[dim], axis=dim)
        cells = jnp.concatenate(
            [
                lax.ppermute(tail, axis, [(i, (i + 1) % count) for i in range(ends)]),
                cells,
                lax.ppermute(head, axis, [((i + 1) % count, i) for i in range(ends)]),
            ],
            axis=dim,
        )
    return cells


def from_behind(value, axis, by):
    size = lax.axis_size(axis)
    pairs = [(i, i + by) for i in range(size) if 0 <= i + by < size]
    return lax.ppermute(value, axis, pairs)


def diffuse(values, row_coef, col_coef):
    row_flux = row_coef[..., :-1, :] * (values[..., 1:, :] - values[..., :-1, :])
    col_flux = col_coef[..., :, :-1] * (values[..., :, 1:] - values[..., :, :-1])
    zeros_row = jnp.zeros_like(values[..., :1, :])
    zeros_col = jnp.zeros_like(values[..., :, :1])
    values = (
        values
        + jnp.concatenate([row_flux, zeros_row], -2)
        - jnp.concatenate([zeros_row, row_flux], -2)
    )
    return (
        values
        + jnp.concatenate([col_flux, zeros_col], -1)
        - jnp.concatenate([zeros_col, col_flux], -1)
    )


def localize(field, coef_band):
    for repeat in range(STEPS):
        widened = padded(field, (("tile", 1),), 1)
        field = diffuse(widened, coef_band[0], coef_band[1])[:, 1:-1]
    return field


def per_device(controls, perturbations, jacobian, obs_weight, radar_mask, row_faces, col_faces):
    row_count = controls.shape[1]
    row_index = lax.axis_index("tile") * row_count + lax.broadcasted_iota(
        jnp.int32, row_faces.shape, 0
    )
    row_coef = jnp.where(
        row_index < row_count * lax.axis_size("tile") - 1, row_faces, jnp.zeros_like(row_faces)
    )
    below_row = from_behind(row_coef[-1:], "tile", 1)
    zero_line = jnp.zeros_like(row_coef[:1])
    row_band = jnp.concatenate([below_row, row_coef, zero_line], 0)
    col_band = jnp.concatenate([zero_line, col_faces, zero_line], 0)
    coef_band = jnp.stack([row_band, col_band])
    localized = localize(controls, coef_band)
    member_sum = jnp.sum(perturbations * localized[:, None], axis=0)
    weights = radar_mask.astype(jnp.float32) * obs_weight
    increment = lax.psum(member_sum, "mem")
    reflect = jnp.sum(jacobian * increment, 0)
    adjoint_inc = jacobian * (weights * reflect)[None]
    sensitivity = jnp.sum(perturbations * adjoint_inc[None], axis=1)
    return controls + localize(sensitivity, coef_band)


def solution(mesh):
    placed = (
        P("mem", "tile", None),
        P("mem", None, "tile", None),
        P(None, "tile", None),
        P("tile", None),
        P("tile", None),
        P("tile", None),
        P("tile", None),
    )
    return jax.shard_map(
        per_device, mesh=mesh, in_specs=placed, out_specs=P("mem", "tile", None), check_vma=False
    )
```

profile of v0, /device:TPU:1, one launch (start us, length us, event | category | flops | bytes accessed | tf_op | source)
XLA Modules:
  0.0 313.1 jit_solution(3506584777765620314)
XLA Ops:
  6.5 1.1 broadcast_select_fusion
  7.6 10.2 %collective-permute-start.2 = (f32[1,1792]{1,0:T(1,128)S(1)}, f32[1,1792]{1,0:T(1,128)S(1)}, u32[]{:S(2)}, u32[]{:S(2)}) collective-permute-start(f32[1,1792]{1,0:T(1,128)S(1)} %slice.228), channel_id=1, source_target_pairs={{0,1},{1,2},{2,3},{3,4},{4,5},{5,6},{6,7},{7,8},{8,9},{9,10},{10,1... | collective-permute-start | bytes 21512 | tf_op jit(solution)/shard_map/ppermute | solution.py:29
  17.8 1.2 fusion.26
  19.1 1.9 collective-permute-start
  21.0 2.4 collective-permute-start.1
  23.4 0.9 pad_maximum_fusion.8
  24.4 8.9 %collective-permute-done.1 = f32[8,1,1792]{2,1,0:T(1,128)S(1)} collective-permute-done((f32[8,1,1792]{2,1,0:T(1,128)S(1)}, f32[8,1,1792]{2,1,0:T(1,128)S(1)}, u32[]{:S(2)}, u32[]{:S(2)}) %collective-permute-start.1) | collective-permute-done | bytes 57376 | tf_op jit(solution)/shard_map/ppermute | solution.py:19
  33.3 0.2 pad_maximum_fusion
  33.5 0.4 fusion.9
  33.9 0.2 fusion.10
  34.2 0.6 pad_subtract_fusion.5
  34.8 1.9 collective-permute-start.3
  36.8 2.4 collective-permute-start.4
  39.3 9.2 %collective-permute-done.4 = f32[8,1,1792]{2,1,0:T(1,128)S(1)} collective-permute-done((f32[8,1,1792]{2,1,0:T(1,128)S(1)}, f32[8,1,1792]{2,1,0:T(1,128)S(1)}, u32[]{:S(2)}, u32[]{:S(2)}) %collective-permute-start.4) | collective-permute-done | bytes 57376 | tf_op jit(solution)/shard_map/ppermute | solution.py:19
  48.5 0.2 pad_maximum_fusion.1
  48.7 0.4 fusion.8
  49.1 0.2 fusion.11
  49.4 0.6 pad_subtract_fusion.4
  50.0 1.9 collective-permute-start.5
  52.0 2.4 collective-permute-start.6
  54.5 8.6 %collective-permute-done.6 = f32[8,1,1792]{2,1,0:T(1,128)S(1)} collective-permute-done((f32[8,1,1792]{2,1,0:T(1,128)S(1)}, f32[8,1,1792]{2,1,0:T(1,128)S(1)}, u32[]{:S(2)}, u32[]{:S(2)}) %collective-permute-start.6) | collective-permute-done | bytes 57376 | tf_op jit(solution)/shard_map/ppermute | solution.py:19
  63.1 0.2 pad_maximum_fusion.2
  63.3 0.4 fusion.7
  63.7 0.2 fusion.12
  64.0 0.6 pad_subtract_fusion.3
  64.7 1.9 collective-permute-start.7
  66.6 2.4 collective-permute-start.8
  69.1 7.1 %collective-permute-done.8 = f32[8,1,1792]{2,1,0:T(1,128)S(1)} collective-permute-done((f32[8,1,1792]{2,1,0:T(1,128)S(1)}, f32[8,1,1792]{2,1,0:T(1,128)S(1)}, u32[]{:S(2)}, u32[]{:S(2)}) %collective-permute-start.8) | collective-permute-done | bytes 57376 | tf_op jit(solution)/shard_map/ppermute | solution.py:19
  76.2 0.2 pad_maximum_fusion.3
  76.4 0.4 fusion.6
  76.9 0.2 fusion.13
  77.1 0.5 pad_subtract_fusion.8
  77.6 1.0 copy-done.1
  78.6 1.2 fusion
  79.8 154.6 %all-reduce.34.cloned.1.call-done = f32[4,16,1792]{2,1,0:T(8,128)} async-done(((f32[4,16,1792]{2,1,0:T(8,128)}), f32[4,16,1792]{2,1,0:T(8,128)}) %all-reduce.34.cloned.1.call-update) | async-done | bytes 458768 | tf_op jit(solution)/shard_map/psum | solution.py:72
  234.4 1.1 multiply_reduce_fusion
  235.5 1.0 multiply_multiply_fusion
  236.5 0.4 fusion.1
  237.0 18.0 %collective-permute-start.9 = (f32[8,1,1792]{2,1,0:T(1,128)S(1)}, f32[8,1,1792]{2,1,0:T(1,128)S(1)}, u32[]{:S(2)}, u32[]{:S(2)}) collective-permute-start(f32[8,1,1792]{2,1,0:T(1,128)S(1)} %get-tuple-element.17), channel_id=1, source_target_pairs={{0,1},{1,2},{2,3},{3,4},{4,5},{5,6},{6,7},{7,8},{8,9},{9,10},{10,1... | collective-permute-start | bytes 172040 | tf_op jit(solution)/shard_map/ppermute | solution.py:17
  255.0 1.9 collective-permute-start.10
  257.0 8.1 %collective-permute-done.10 = f32[8,1,1792]{2,1,0:T(1,128)S(1)} collective-permute-done((f32[8,1,1792]{2,1,0:T(1,128)S(1)}, f32[8,1,1792]{2,1,0:T(1,128)S(1)}, u32[]{:S(2)}, u32[]{:S(2)}) %collective-permute-start.10) | collective-permute-done | bytes 57376 | tf_op jit(solution)/shard_map/ppermute | solution.py:19
  265.0 0.2 pad_maximum_fusion.4
  265.2 0.4 fusion.5
  265.7 0.2 fusion.14
  265.9 0.6 pad_subtract_fusion.2
  266.6 1.9 collective-permute-start.11
  268.5 2.4 collective-permute-start.12
  271.0 7.1 %collective-permute-done.12 = f32[8,1,1792]{2,1,0:T(1,128)S(1)} collective-permute-done((f32[8,1,1792]{2,1,0:T(1,128)S(1)}, f32[8,1,1792]{2,1,0:T(1,128)S(1)}, u32[]{:S(2)}, u32[]{:S(2)}) %collective-permute-start.12) | collective-permute-done | bytes 57376 | tf_op jit(solution)/shard_map/ppermute | solution.py:19
  278.2 0.2 pad_maximum_fusion.5
  278.4 0.4 fusion.4
  278.8 0.2 fusion.15
  279.0 0.6 pad_subtract_fusion.1
  279.7 1.9 collective-permute-start.13
  281.7 2.6 collective-permute-start.14
  284.4 6.7 %collective-permute-done.14 = f32[8,1,1792]{2,1,0:T(1,128)S(1)} collective-permute-done((f32[8,1,1792]{2,1,0:T(1,128)S(1)}, f32[8,1,1792]{2,1,0:T(1,128)S(1)}, u32[]{:S(2)}, u32[]{:S(2)}) %collective-permute-start.14) | collective-permute-done | bytes 57376 | tf_op jit(solution)/shard_map/ppermute | solution.py:19
  291.3 0.4 fusion.3
  291.7 0.2 fusion.16
  292.0 0.6 pad_subtract_fusion
  292.7 1.9 collective-permute-start.15
  294.6 2.4 collective-permute-start.16
  297.1 6.9 %collective-permute-done.16 = f32[8,1,1792]{2,1,0:T(1,128)S(1)} collective-permute-done((f32[8,1,1792]{2,1,0:T(1,128)S(1)}, f32[8,1,1792]{2,1,0:T(1,128)S(1)}, u32[]{:S(2)}, u32[]{:S(2)}) %collective-permute-start.16) | collective-permute-done | bytes 57376 | tf_op jit(solution)/shard_map/ppermute | solution.py:19
  304.2 0.4 fusion.2
  304.6 0.2 fusion.17
  304.9 1.4 fusion.18
  (36 shorter events, 1.6 us)
Async XLA Ops:
  6.5 26.8 %copy-start = (f32[8,16,1792]{2,1,0:T(8,128)S(1)}, f32[8,16,1792]{2,1,0:T(8,128)}, u32[]{:S(2)}) copy-start(f32[8,16,1792]{2,1,0:T(8,128)} %param.7) | copy-start | bytes 2752516
  6.5 227.9 %all-reduce.34.cloned.1.call-start = ((), (), s32[]{:S(2)}) async-start(), calls=%async_computation | async-start | bytes 917504 | tf_op jit(solution)/shard_map/psum | solution.py:72
  7.6 16.7 %collective-permute-start.2 = (f32[1,1792]{1,0:T(1,128)S(1)}, f32[1,1792]{1,0:T(1,128)S(1)}, u32[]{:S(2)}, u32[]{:S(2)}) collective-permute-start(f32[1,1792]{1,0:T(1,128)S(1)} %slice.228), channel_id=1, source_target_pairs={{0,1},{1,2},{2,3},{3,4},{4,5},{5,6},{6,7},{7,8},{8,9},{9,10},{10,1... | collective-permute-start | bytes 21512 | tf_op jit(solution)/shard_map/ppermute | solution.py:29
  19.1 5.3 %collective-permute-start = (f32[8,1,1792]{2,1,0:T(1,128)S(1)}, f32[8,1,1792]{2,1,0:T(1,128)S(1)}, u32[]{:S(2)}, u32[]{:S(2)}) collective-permute-start(f32[8,1,1792]{2,1,0:T(1,128)S(1)} %get-tuple-element.19), channel_id=1, source_target_pairs={{0,1},{1,2},{2,3},{3,4},{4,5},{5,6},{6,7},{7,8},{8,9},{9,10},{10,1... | collective-permute-start | bytes 172040 | tf_op jit(solution)/shard_map/ppermute | solution.py:17
  21.0 12.3 %collective-permute-start.1 = (f32[8,1,1792]{2,1,0:T(1,128)S(1)}, f32[8,1,1792]{2,1,0:T(1,128)S(1)}, u32[]{:S(2)}, u32[]{:S(2)}) collective-permute-start(f32[8,1,1792]{2,1,0:T(1,128)S(1)} %get-tuple-element.20), channel_id=1, source_target_pairs={{1,0},{2,1},{3,2},{4,3},{5,4},{6,5},{7,6},{8,7},{9,8},{10,9},{11,1... | collective-permute-start | bytes 172040 | tf_op jit(solution)/shard_map/ppermute | solution.py:19
  34.8 4.4 %collective-permute-start.3 = (f32[8,1,1792]{2,1,0:T(1,128)S(1)}, f32[8,1,1792]{2,1,0:T(1,128)S(1)}, u32[]{:S(2)}, u32[]{:S(2)}) collective-permute-start(f32[8,1,1792]{2,1,0:T(1,128)S(1)} %get-tuple-element.15), channel_id=1, source_target_pairs={{0,1},{1,2},{2,3},{3,4},{4,5},{5,6},{6,7},{7,8},{8,9},{9,10},{10,1... | collective-permute-start | bytes 172040 | tf_op jit(solution)/shard_map/ppermute | solution.py:17
  36.8 11.7 %collective-permute-start.4 = (f32[8,1,1792]{2,1,0:T(1,128)S(1)}, f32[8,1,1792]{2,1,0:T(1,128)S(1)}, u32[]{:S(2)}, u32[]{:S(2)}) collective-permute-start(f32[8,1,1792]{2,1,0:T(1,128)S(1)} %get-tuple-element.16), channel_id=1, source_target_pairs={{1,0},{2,1},{3,2},{4,3},{5,4},{6,5},{7,6},{8,7},{9,8},{10,9},{11,1... | collective-permute-start | bytes 172040 | tf_op jit(solution)/shard_map/ppermute | solution.py:19
  50.0 4.4 %collective-permute-start.5 = (f32[8,1,1792]{2,1,0:T(1,128)S(1)}, f32[8,1,1792]{2,1,0:T(1,128)S(1)}, u32[]{:S(2)}, u32[]{:S(2)}) collective-permute-start(f32[8,1,1792]{2,1,0:T(1,128)S(1)} %get-tuple-element.13), channel_id=1, source_target_pairs={{0,1},{1,2},{2,3},{3,4},{4,5},{5,6},{6,7},{7,8},{8,9},{9,10},{10,1... | collective-permute-start | bytes 172040 | tf_op jit(solution)/shard_map/ppermute | solution.py:17
  52.0 11.1 %collective-permute-start.6 = (f32[8,1,1792]{2,1,0:T(1,128)S(1)}, f32[8,1,1792]{2,1,0:T(1,128)S(1)}, u32[]{:S(2)}, u32[]{:S(2)}) collective-permute-start(f32[8,1,1792]{2,1,0:T(1,128)S(1)} %get-tuple-element.14), channel_id=1, source_target_pairs={{1,0},{2,1},{3,2},{4,3},{5,4},{6,5},{7,6},{8,7},{9,8},{10,9},{11,1... | collective-permute-start | bytes 172040 | tf_op jit(solution)/shard_map/ppermute | solution.py:19
  64.7 4.4 %collective-permute-start.7 = (f32[8,1,1792]{2,1,0:T(1,128)S(1)}, f32[8,1,1792]{2,1,0:T(1,128)S(1)}, u32[]{:S(2)}, u32[]{:S(2)}) collective-permute-start(f32[8,1,1792]{2,1,0:T(1,128)S(1)} %get-tuple-element.11), channel_id=1, source_target_pairs={{0,1},{1,2},{2,3},{3,4},{4,5},{5,6},{6,7},{7,8},{8,9},{9,10},{10,1... | collective-permute-start | bytes 172040 | tf_op jit(solution)/shard_map/ppermute | solution.py:17
  66.6 9.6 %collective-permute-start.8 = (f32[8,1,1792]{2,1,0:T(1,128)S(1)}, f32[8,1,1792]{2,1,0:T(1,128)S(1)}, u32[]{:S(2)}, u32[]{:S(2)}) collective-permute-start(f32[8,1,1792]{2,1,0:T(1,128)S(1)} %get-tuple-element.12), channel_id=1, source_target_pairs={{1,0},{2,1},{3,2},{4,3},{5,4},{6,5},{7,6},{8,7},{9,8},{10,9},{11,1... | collective-permute-start | bytes 172040 | tf_op jit(solution)/shard_map/ppermute | solution.py:19
  77.1 1.5 copy-start.1
  78.6 155.8 %copy-start.2 = (f32[4,16,1792]{2,1,0:T(8,128)S(1)}, f32[4,16,1792]{2,1,0:T(8,128)}, u32[]{:S(2)}) copy-start(f32[4,16,1792]{2,1,0:T(8,128)} %param.9) | copy-start | bytes 1376260
  237.0 20.0 %collective-permute-start.9 = (f32[8,1,1792]{2,1,0:T(1,128)S(1)}, f32[8,1,1792]{2,1,0:T(1,128)S(1)}, u32[]{:S(2)}, u32[]{:S(2)}) collective-permute-start(f32[8,1,1792]{2,1,0:T(1,128)S(1)} %get-tuple-element.17), channel_id=1, source_target_pairs={{0,1},{1,2},{2,3},{3,4},{4,5},{5,6},{6,7},{7,8},{8,9},{9,10},{10,1... | collective-permute-start | bytes 172040 | tf_op jit(solution)/shard_map/ppermute | solution.py:17
  255.0 10.0 %collective-permute-start.10 = (f32[8,1,1792]{2,1,0:T(1,128)S(1)}, f32[8,1,1792]{2,1,0:T(1,128)S(1)}, u32[]{:S(2)}, u32[]{:S(2)}) collective-permute-start(f32[8,1,1792]{2,1,0:T(1,128)S(1)} %get-tuple-element.18), channel_id=1, source_target_pairs={{1,0},{2,1},{3,2},{4,3},{5,4},{6,5},{7,6},{8,7},{9,8},{10,9},{11,1... | collective-permute-start | bytes 172040 | tf_op jit(solution)/shard_map/ppermute | solution.py:19
  266.6 4.4 %collective-permute-start.11 = (f32[8,1,1792]{2,1,0:T(1,128)S(1)}, f32[8,1,1792]{2,1,0:T(1,128)S(1)}, u32[]{:S(2)}, u32[]{:S(2)}) collective-permute-start(f32[8,1,1792]{2,1,0:T(1,128)S(1)} %get-tuple-element.9), channel_id=1, source_target_pairs={{0,1},{1,2},{2,3},{3,4},{4,5},{5,6},{6,7},{7,8},{8,9},{9,10},{10,1... | collective-permute-start | bytes 172040 | tf_op jit(solution)/shard_map/ppermute | solution.py:17
  268.5 9.6 %collective-permute-start.12 = (f32[8,1,1792]{2,1,0:T(1,128)S(1)}, f32[8,1,1792]{2,1,0:T(1,128)S(1)}, u32[]{:S(2)}, u32[]{:S(2)}) collective-permute-start(f32[8,1,1792]{2,1,0:T(1,128)S(1)} %get-tuple-element.10), channel_id=1, source_target_pairs={{1,0},{2,1},{3,2},{4,3},{5,4},{6,5},{7,6},{8,7},{9,8},{10,9},{11,1... | collective-permute-start | bytes 172040 | tf_op jit(solution)/shard_map/ppermute | solution.py:19
  279.7 4.6 %collective-permute-start.13 = (f32[8,1,1792]{2,1,0:T(1,128)S(1)}, f32[8,1,1792]{2,1,0:T(1,128)S(1)}, u32[]{:S(2)}, u32[]{:S(2)}) collective-permute-start(f32[8,1,1792]{2,1,0:T(1,128)S(1)} %get-tuple-element.7), channel_id=1, source_target_pairs={{0,1},{1,2},{2,3},{3,4},{4,5},{5,6},{6,7},{7,8},{8,9},{9,10},{10,1... | collective-permute-start | bytes 172040 | tf_op jit(solution)/shard_map/ppermute | solution.py:17
  281.7 9.4 %collective-permute-start.14 = (f32[8,1,1792]{2,1,0:T(1,128)S(1)}, f32[8,1,1792]{2,1,0:T(1,128)S(1)}, u32[]{:S(2)}, u32[]{:S(2)}) collective-permute-start(f32[8,1,1792]{2,1,0:T(1,128)S(1)} %get-tuple-element.8), channel_id=1, source_target_pairs={{1,0},{2,1},{3,2},{4,3},{5,4},{6,5},{7,6},{8,7},{9,8},{10,9},{11,1... | collective-permute-start | bytes 172040 | tf_op jit(solution)/shard_map/ppermute | solution.py:19
  292.7 4.4 %collective-permute-start.15 = (f32[8,1,1792]{2,1,0:T(1,128)S(1)}, f32[8,1,1792]{2,1,0:T(1,128)S(1)}, u32[]{:S(2)}, u32[]{:S(2)}) collective-permute-start(f32[8,1,1792]{2,1,0:T(1,128)S(1)} %get-tuple-element.5), channel_id=1, source_target_pairs={{0,1},{1,2},{2,3},{3,4},{4,5},{5,6},{6,7},{7,8},{8,9},{9,10},{10,1... | collective-permute-start | bytes 172040 | tf_op jit(solution)/shard_map/ppermute | solution.py:17
  294.6 9.4 %collective-permute-start.16 = (f32[8,1,1792]{2,1,0:T(1,128)S(1)}, f32[8,1,1792]{2,1,0:T(1,128)S(1)}, u32[]{:S(2)}, u32[]{:S(2)}) collective-permute-start(f32[8,1,1792]{2,1,0:T(1,128)S(1)} %get-tuple-element.6), channel_id=1, source_target_pairs={{1,0},{2,1},{3,2},{4,3},{5,4},{6,5},{7,6},{8,7},{9,8},{10,9},{11,1... | collective-permute-start | bytes 172040 | tf_op jit(solution)/shard_map/ppermute | solution.py:19
Sparse Core Ops, SparseCore 0:
  79.9 154.3 all-reduce.33
where the time goes:
time: 314 us; the launch traced here: 313 us
  waiting for transfers between devices  217 us (69%)
  starting transfers between devices  60.6 us (19%)
  other arithmetic  18.1 us (6%)
  between operations  13.9 us (4%)
  local copies, waits for them, and re-layouts  3.29 us (1%)
    psum x1, waiting for transfers between devices, per_device(): increment = lax.psum(member_sum, 'mem')  155 us
    ppermute x8, waiting for transfers between devices, padded(): lax.ppermute(head, axis, [((i + 1) % count, i) for i in range(ends)])  62.7 us
    ppermute x8, starting transfers between devices, padded(): lax.ppermute(tail, axis, [(i, (i + 1) % count) for i in range(ends)])  31.5 us
    ppermute x8, starting transfers between devices, padded(): lax.ppermute(head, axis, [((i + 1) % count, i) for i in range(ends)])  18.9 us
    ppermute x1, starting transfers between devices, from_behind(): return lax.ppermute(value, axis, pairs)  10.2 us
  transfers between devices with their start and end apart: 18, of which 9 were waited for; matrix products, arithmetic and copies ran while one was open for 1% of the time, Pallas kernels for 0%

commit v1 on v0

v1 whole, which is shorter than its diff:
```python
import jax
import jax.numpy as jnp
from jax import lax
from jax.experimental import pallas as pl
from jax.experimental.pallas import tpu as pltpu
from jax.sharding import PartitionSpec as P

MEM = 16
TILE = 32
H = 4
MESH = pl.DeviceIdType.MESH
f32 = jnp.float32


def kernel(ctl, pert, jac, obs, msk, rf, cf, out,
           C, A, B, Q, K, KR, KC, Pv, Jv, nat, natm, part, recv, rown, R, Rup, Rdn, O,
           lsem, csem, osem, hs, hr, ss, sr):
    G = Q.shape[1]
    n = Q.shape[2]
    E = Q.shape[0]
    rows = E - 2 * H
    m = lax.axis_index("mem")
    t = lax.axis_index("tile")
    x = m // 4
    z = m % 4
    has_up = t > 0
    has_dn = t < TILE - 1

    bar = pltpu.get_barrier_semaphore()

    def greet(mm, tt):
        pl.semaphore_signal(bar, inc=1, device_id=(mm, tt), device_id_type=MESH)

    def ring(i, carry):
        greet((m + i) % MEM, t)
        return carry

    def side(tt, full_z, own_z):
        @pl.when(z == full_z)
        def _():
            def body(i, carry):
                greet(i, tt)
                return carry
            lax.fori_loop(0, MEM, body, 0)

        @pl.when(z != full_z)
        def _():
            def body(i, carry):
                greet(i * 4 + own_z, tt)
                return carry
            lax.fori_loop(0, 4, body, 0)

            @pl.when(z != own_z)
            def _():
                greet(m, tt)

    lax.fori_loop(1, MEM, ring, 0)

    @pl.when(has_up)
    def _():
        side(t - 1, 0, 3)

    @pl.when(has_dn)
    def _():
        side(t + 1, 3, 0)

    loads = [
        pltpu.make_async_copy(pert, Pv, lsem.at[0]),
        pltpu.make_async_copy(jac, Jv, lsem.at[1]),
        pltpu.make_async_copy(rf, nat.at[0], lsem.at[2]),
        pltpu.make_async_copy(cf, nat.at[1], lsem.at[3]),
        pltpu.make_async_copy(obs, nat.at[2], lsem.at[4]),
        pltpu.make_async_copy(msk, natm, lsem.at[5]),
    ]
    for cp in loads:
        cp.start()

    def cload(r):
        return pltpu.make_async_copy(ctl.at[:, r, :], C.at[1 + H + r], csem.at[r])

    for r in range(rows):
        cload(r).start()

    zero = jnp.zeros((G, n), f32)
    for e in list(range(0, H + 1)) + list(range(H + rows + 1, E + 2)):
        C[e] = zero
        A[e] = zero
        B[e] = zero
    for e in (0, E + 1):
        KR[e] = zero
        KC[e] = zero
    line = jnp.zeros((1, n), f32)

    @pl.when(jnp.logical_not(has_up))
    def _():
        for e in range(H):
            Q[e] = zero
            for i in range(3):
                K[i, e] = line
        for e in range(2 * H):
            Rup[e] = line

    @pl.when(jnp.logical_not(has_dn))
    def _():
        for e in range(H + rows, E):
            Q[e] = zero
            for i in range(3):
                K[i, e] = line
        for e in range(2 * H):
            Rdn[e] = line

    for cp in loads[2:]:
        cp.wait()
    last = jnp.where(has_dn, 1.0, 0.0).astype(f32)
    lane = lax.broadcasted_iota(jnp.int32, (1, n), 1)
    for r in range(rows):
        row = nat[0, r:r + 1, :]
        K[0, H + r] = row * last if r == rows - 1 else row
        K[1, H + r] = jnp.where(lane < n - 1, nat[1, r:r + 1, :], 0.0)
        K[2, H + r] = nat[2, r:r + 1, :] * natm[r:r + 1, :].astype(f32)

    loads[0].wait()
    loads[1].wait()

    def qtile(j, carry):
        cols = pl.ds(pl.multiple_of(j * 128, 128), 128)
        q = Pv[:, 0, :, cols].astype(f32) * Jv[0, :, cols][None]
        for v in range(1, 4):
            q = q + Pv[:, v, :, cols].astype(f32) * Jv[v, :, cols][None]
        Q[H:H + rows, :, cols] = jnp.swapaxes(q, 0, 1)
        return carry

    lax.fori_loop(0, n // 128, qtile, 0)

    near = jnp.where(z == 0, 16, jnp.where(z == 3, 4, 5))
    far = jnp.where(z == 3, 16, jnp.where(z == 0, 4, 5))
    pl.semaphore_wait(bar, MEM - 1 + jnp.where(has_up, near, 0) + jnp.where(has_dn, far, 0))

    def halo(buf, up, i):
        if buf is K:
            src = K.at[:, pl.ds(H if up else rows, H)]
            dst = K.at[:, pl.ds(H + rows if up else 0, H)]
        else:
            src = Q.at[pl.ds(H if up else rows, H)]
            dst = Q.at[pl.ds(H + rows if up else 0, H)]
        return pltpu.make_async_remote_copy(
            src, dst, hs.at[i], hr.at[i], device_id=(m, t - 1 if up else t + 1), device_id_type=MESH)

    @pl.when(has_up)
    def _():
        halo(K, True, 0).start()
        halo(Q, True, 2).start()

    @pl.when(has_dn)
    def _():
        halo(K, False, 1).start()
        halo(Q, False, 3).start()

    def widen(e, carry):
        KR[1 + e] = jnp.broadcast_to(K[0, e], (G, n))
        KC[1 + e] = jnp.broadcast_to(K[1, e], (G, n))
        return carry

    lax.fori_loop(H, H + rows, widen, 0)
    for r in range(rows):
        cload(r).wait()

    @pl.when(has_up)
    def _():
        halo(K, False, 1).wait_recv()

    @pl.when(has_dn)
    def _():
        halo(K, True, 0).wait_recv()

    lax.fori_loop(0, H, widen, 0)
    lax.fori_loop(H + rows, E, widen, 0)

    def stencil(src, e):
        v = src[1 + e]
        down = KR[1 + e] * (src[2 + e] - v)
        up = KR[e] * (v - src[e])
        flux = KC[1 + e] * (pltpu.roll(v, n - 1, 1) - v)
        return v + (down - up) + (flux - pltpu.roll(flux, 1, 1))

    def step(src, dst, lo, hi):
        def body(e, carry):
            dst[1 + e] = stencil(src, e)
            return carry
        lax.fori_loop(lo, hi, body, 0)

    step(C, A, H - 1, H + rows + 1)
    step(A, B, H - 2, H + rows + 2)
    step(B, A, H - 3, H + rows + 3)
    step(A, B, 0, E)

    def product(e, carry):
        part[e] = jnp.sum(B[1 + e] * Q[e], axis=0, keepdims=True)
        return carry

    lax.fori_loop(H, H + rows, product, 0)

    @pl.when(has_up)
    def _():
        halo(Q, False, 3).wait_recv()

    @pl.when(has_dn)
    def _():
        halo(Q, True, 2).wait_recv()

    lax.fori_loop(0, H, product, 0)
    lax.fori_loop(H + rows, E, product, 0)

    def owned(zz, xx):
        return ((2 * xx, 2), (8 + xx, 1), (12 + xx, 1), (16 + 2 * xx, 2))[zz]

    def scatter(i, carry):
        xx = (x + i) % 4
        for zz in range(4):
            start, count = owned(zz, xx)

            @pl.when(jnp.logical_or(xx != x, z != zz))
            def _():
                pltpu.make_async_remote_copy(
                    part.at[pl.ds(start, count)], recv.at[m, pl.ds(0, count)], ss.at[0], sr.at[0],
                    device_id=(xx * 4 + zz, t), device_id_type=MESH).start()
        return carry

    lax.fori_loop(0, 4, scatter, 0)

    peer = (m + 1) % MEM

    def waiter(ref, sems):
        return pltpu.make_async_remote_copy(ref, ref, sems[0], sems[1], device_id=(peer, t), device_id_type=MESH)

    rs = (ss.at[0], sr.at[0])
    ag = (ss.at[1], sr.at[1])
    nu = (ss.at[2], sr.at[2])
    nd = (ss.at[3], sr.at[3])
    for zz in range(4):
        start, count = owned(zz, x)

        @pl.when(z == zz)
        def _():
            recv[m, 0:count] = part[pl.ds(start, count)]
            waiter(recv.at[pl.ds(0, MEM - 1), pl.ds(0, count)], rs).wait_recv()
            total = recv[0, 0:count]
            for i in range(1, MEM):
                total = total + recv[i, 0:count]
            rown[0:count] = total
            R[pl.ds(start, count)] = total

            def gather(i, carry):
                pltpu.make_async_remote_copy(
                    rown.at[pl.ds(0, count)], R.at[pl.ds(start, count)], ag[0], ag[1],
                    device_id=((m + i) % MEM, t), device_id_type=MESH).start()
                return carry

            if zz in (0, 3):
                near = has_up if zz == 0 else has_dn
                sem = nu if zz == 0 else nd
                dst = Rdn if zz == 0 else Rup

                @pl.when(near)
                def _():
                    def cross(i, carry):
                        pltpu.make_async_remote_copy(
                            rown.at[pl.ds(0, 2)], dst.at[pl.ds(2 * x, 2)], sem[0], sem[1],
                            device_id=((m + i) % MEM, t - 1 if zz == 0 else t + 1), device_id_type=MESH).start()
                        return carry
                    lax.fori_loop(0, MEM, cross, 0)

            lax.fori_loop(1, MEM, gather, 0)
            waiter(R.at[pl.ds(0, E - count)], ag).wait_recv()

    @pl.when(has_up)
    def _():
        waiter(Rup, nd).wait_recv()

    @pl.when(has_dn)
    def _():
        waiter(Rdn, nu).wait_recv()

    def spread(e, extra):
        r = R[e]
        if extra is not None:
            r = r + extra
        A[1 + e] = Q[e] * jnp.broadcast_to(K[2, e] * r, (G, n))

    def spread_up(e, carry):
        spread(e, Rup[e])
        return carry

    def spread_mid(e, carry):
        spread(e, None)
        return carry

    def spread_dn(e, carry):
        spread(e, Rdn[e - rows])
        return carry

    lax.fori_loop(0, 2 * H, spread_up, 0)
    lax.fori_loop(2 * H, rows, spread_mid, 0)
    lax.fori_loop(rows, E, spread_dn, 0)
    step(A, B, 1, E - 1)
    step(B, A, 2, E - 2)
    step(A, B, 3, E - 3)

    def store(r):
        return pltpu.make_async_copy(O.at[r], out.at[:, r, :], osem.at[r])

    def final(r, carry):
        O[r] = C[1 + H + r] + stencil(B, H + r)
        return carry

    for r in range(rows):
        final(r, 0)
        store(r).start()

    @pl.when(has_up)
    def _():
        halo(K, True, 0).wait_send()
        halo(Q, True, 2).wait_send()

    @pl.when(has_dn)
    def _():
        halo(K, False, 1).wait_send()
        halo(Q, False, 3).wait_send()

    for zz in range(4):
        count = owned(zz, 0)[1]

        @pl.when(z == zz)
        def _():
            waiter(part.at[pl.ds(0, E - count)], rs).wait_send()
            waiter(recv.at[pl.ds(0, MEM - 1), pl.ds(0, count)], ag).wait_send()
            if zz in (0, 3):
                @pl.when(has_up if zz == 0 else has_dn)
                def _():
                    waiter(recv, nu if zz == 0 else nd).wait_send()

    for r in range(rows):
        store(r).wait()


def per_device(controls, perturbations, jacobian, obs_weight, radar_mask, row_faces, col_faces):
    G, rows, n = controls.shape
    E = rows + 2 * H
    big = pltpu.VMEM((E + 2, G, n), f32)
    row = lambda *s: pltpu.VMEM(s + (1, n), f32)
    dma = pltpu.SemaphoreType.DMA
    return pl.pallas_call(
        kernel,
        out_shape=jax.ShapeDtypeStruct(controls.shape, f32),
        in_specs=[pl.BlockSpec(memory_space=pl.ANY)] * 7,
        out_specs=pl.BlockSpec(memory_space=pl.ANY),
        scratch_shapes=[
            big, big, big, pltpu.VMEM((E, G, n), f32), row(3, E), big, big,
            pltpu.VMEM(perturbations.shape, jnp.bfloat16), pltpu.VMEM(jacobian.shape, f32),
            pltpu.VMEM((3, rows, n), f32), pltpu.VMEM((rows, n), jnp.int32),
            row(E), row(MEM, 2), row(2), row(E), row(2 * H), row(2 * H),
            pltpu.VMEM((rows, G, n), f32),
            dma((6,)), dma((rows,)), dma((rows,)), dma((4,)), dma((4,)), dma((4,)), dma((4,)),
        ],
        compiler_params=pltpu.CompilerParams(
            collective_id=0, has_side_effects=True, vmem_limit_bytes=40 * 1024 * 1024),
    )(controls, perturbations, jacobian, obs_weight, radar_mask, row_faces, col_faces)


def solution(mesh):
    placed = (
        P("mem", "tile", None),
        P("mem", None, "tile", None),
        P(None, "tile", None),
        P("tile", None),
        P("tile", None),
        P("tile", None),
        P("tile", None),
    )
    return jax.shard_map(
        per_device, mesh=mesh, in_specs=placed, out_specs=P("mem", "tile", None), check_vma=False
    )
```

time: 314 us -> 78.5 us (0.25)
  the two profiles are of different devices: /device:TPU:1 before, /device:TPU:24 now
where the time goes in v1:
time: 78.5 us; the launch traced here: 78.2 us
  Pallas kernels  70 us (89%)
  local copies, waits for them, and re-layouts  8.21 us (10%)
    pallas_call x1, Pallas kernels, per_device(): pl.pallas_call(kernel, out_shape=jax.ShapeDtypeStruct(controls.shape, f32...  70 us
    unnamed x15, local copies, waits for them, and re-layouts  8.21 us

profile of v1, /device:TPU:24, one launch (start us, length us, event | category | flops | bytes accessed | tf_op | source)
XLA Modules:
  0.0 78.2 jit_solution(6093049505363483941)
XLA Ops:
  0.0 0.0 copy-start
  0.0 1.5 %copy-done = bf16[8,4,16,1792]{3,2,1,0:T(8,128)(2,1)S(1)} copy-done((bf16[8,4,16,1792]{3,2,1,0:T(8,128)(2,1)S(1)}, bf16[8,4,16,1792]{3,2,1,0:T(8,128)(2,1)}, u32[]{:S(2)}) %copy-start) | copy-done | bytes 1835032
  1.5 0.0 copy-start.1
  1.5 1.2 %copy-done.1 = f32[8,16,1792]{2,1,0:T(8,128)S(1)} copy-done((f32[8,16,1792]{2,1,0:T(8,128)S(1)}, f32[8,16,1792]{2,1,0:T(8,128)}, u32[]{:S(2)}) %copy-start.1) | copy-done | bytes 917528
  2.7 0.0 copy-start.2
  2.7 1.0 %copy-done.2 = f32[4,16,1792]{2,1,0:T(8,128)S(1)} copy-done((f32[4,16,1792]{2,1,0:T(8,128)S(1)}, f32[4,16,1792]{2,1,0:T(8,128)}, u32[]{:S(2)}) %copy-start.2) | copy-done | bytes 458776
  3.7 0.0 copy-start.3
  3.7 0.9 %copy-done.3 = f32[16,1792]{1,0:T(8,128)S(1)} copy-done((f32[16,1792]{1,0:T(8,128)S(1)}, f32[16,1792]{1,0:T(8,128)}, u32[]{:S(2)}) %copy-start.3) | copy-done | bytes 114712
  4.6 0.0 copy-start.4
  4.6 0.9 %copy-done.4 = s32[16,1792]{1,0:T(8,128)S(1)} copy-done((s32[16,1792]{1,0:T(8,128)S(1)}, s32[16,1792]{1,0:T(8,128)}, u32[]{:S(2)}) %copy-start.4) | copy-done | bytes 114712
  5.5 0.0 copy-start.5
  5.5 0.9 %copy-done.5 = f32[16,1792]{1,0:T(8,128)S(1)} copy-done((f32[16,1792]{1,0:T(8,128)S(1)}, f32[16,1792]{1,0:T(8,128)}, u32[]{:S(2)}) %copy-start.5) | copy-done | bytes 114712
  6.4 0.0 copy-start.6
  6.4 0.9 %copy-done.6 = f32[16,1792]{1,0:T(8,128)S(1)} copy-done((f32[16,1792]{1,0:T(8,128)S(1)}, f32[16,1792]{1,0:T(8,128)}, u32[]{:S(2)}) %copy-start.6) | copy-done | bytes 114712
  7.3 70.0 %shard_map.73 = f32[8,16,1792]{2,1,0:T(8,128)S(1)} custom-call(f32[8,16,1792]{2,1,0:T(8,128)S(1)} %copy-done.1, bf16[8,4,16,1792]{3,2,1,0:T(8,128)(2,1)S(1)} %copy-done, f32[4,16,1792]{2,1,0:T(8,128)S(1)} %copy-done.2, f32[16,1792]{1,0:T(8,128)S(1)} %copy-done.3, s32[16,1792]{1,0:T(8,128)S(1)} %copy-done.4, f32[16,1792]{1,0:T(8,128)S(1)} %copy-done.5, ...), custom_call_target="tpu_custom_call" | custom-call | tf_op jit(solution)/shard_map/pallas_call | solution.py:352
  77.3 0.9 %copy.9 = f32[8,16,1792]{2,1,0:T(8,128)} copy(f32[8,16,1792]{2,1,0:T(8,128)S(1)} %shard_map.73) | data formatting | bytes 1835008
Async XLA Ops:
  0.0 1.5 %copy-start = (bf16[8,4,16,1792]{3,2,1,0:T(8,128)(2,1)S(1)}, bf16[8,4,16,1792]{3,2,1,0:T(8,128)(2,1)}, u32[]{:S(2)}) copy-start(bf16[8,4,16,1792]{3,2,1,0:T(8,128)(2,1)} %pert.1) | copy-start | bytes 5505028
  1.5 1.2 %copy-start.1 = (f32[8,16,1792]{2,1,0:T(8,128)S(1)}, f32[8,16,1792]{2,1,0:T(8,128)}, u32[]{:S(2)}) copy-start(f32[8,16,1792]{2,1,0:T(8,128)} %ctl.1) | copy-start | bytes 2752516
  2.7 1.0 %copy-start.2 = (f32[4,16,1792]{2,1,0:T(8,128)S(1)}, f32[4,16,1792]{2,1,0:T(8,128)}, u32[]{:S(2)}) copy-start(f32[4,16,1792]{2,1,0:T(8,128)} %jac.1) | copy-start | bytes 1376260
  3.7 0.9 %copy-start.3 = (f32[16,1792]{1,0:T(8,128)S(1)}, f32[16,1792]{1,0:T(8,128)}, u32[]{:S(2)}) copy-start(f32[16,1792]{1,0:T(8,128)} %obs.1) | copy-start | bytes 344068
  4.6 0.9 %copy-start.4 = (s32[16,1792]{1,0:T(8,128)S(1)}, s32[16,1792]{1,0:T(8,128)}, u32[]{:S(2)}) copy-start(s32[16,1792]{1,0:T(8,128)} %msk.1) | copy-start | bytes 344068
  5.5 0.9 %copy-start.5 = (f32[16,1792]{1,0:T(8,128)S(1)}, f32[16,1792]{1,0:T(8,128)}, u32[]{:S(2)}) copy-start(f32[16,1792]{1,0:T(8,128)} %rf.1) | copy-start | bytes 344068
  6.4 0.9 %copy-start.6 = (f32[16,1792]{1,0:T(8,128)S(1)}, f32[16,1792]{1,0:T(8,128)}, u32[]{:S(2)}) copy-start(f32[16,1792]{1,0:T(8,128)} %cf.1) | copy-start | bytes 344068

commit v2 on v1

--- a/solution.py
+++ b/solution.py
@@ -10,11 +10,12 @@
 H = 4
 MESH = pl.DeviceIdType.MESH
 f32 = jnp.float32
+UA, UB, UC, UD, UE = 9, 5, 11, 8, 8
 
 
 def kernel(ctl, pert, jac, obs, msk, rf, cf, out,
-           C, A, B, Q, K, KR, KC, Pv, Jv, nat, natm, part, recv, rown, R, Rup, Rdn, O,
-           lsem, csem, osem, hs, hr, ss, sr):
+           C, A, B, Q, K, KR, KC, KL, Pv, Jv, nat, natm, part, recv, rown, R, Rup, Rdn, O,
+           lsem, psem, csem, osem, hs, hr, fs, fr, ss, sr):
     G = Q.shape[1]
     n = Q.shape[2]
     E = Q.shape[0]
@@ -54,32 +55,128 @@
             def _():
                 greet(m, tt)
 
-    lax.fori_loop(1, MEM, ring, 0)
-
-    @pl.when(has_up)
-    def _():
-        side(t - 1, 0, 3)
-
-    @pl.when(has_dn)
-    def _():
-        side(t + 1, 3, 0)
-
-    loads = [
-        pltpu.make_async_copy(pert, Pv, lsem.at[0]),
-        pltpu.make_async_copy(jac, Jv, lsem.at[1]),
-        pltpu.make_async_copy(rf, nat.at[0], lsem.at[2]),
-        pltpu.make_async_copy(cf, nat.at[1], lsem.at[3]),
-        pltpu.make_async_copy(obs, nat.at[2], lsem.at[4]),
-        pltpu.make_async_copy(msk, natm, lsem.at[5]),
+    step_cols = 256
+    parts = n // step_cols
+    small = [
+        pltpu.make_async_copy(rf, nat.at[0], lsem.at[0]),
+        pltpu.make_async_copy(cf, nat.at[1], lsem.at[1]),
+        pltpu.make_async_copy(obs, nat.at[2], lsem.at[2]),
+        pltpu.make_async_copy(msk, natm, lsem.at[3]),
     ]
-    for cp in loads:
-        cp.start()
+    jload = pltpu.make_async_copy(jac, Jv, lsem.at[4])
+
+    def pload(i):
+        cols = pl.ds(i * step_cols, step_cols)
+        return pltpu.make_async_copy(pert.at[:, :, :, cols], Pv.at[:, :, :, cols], psem.at[i])
 
     def cload(r):
         return pltpu.make_async_copy(ctl.at[:, r, :], C.at[1 + H + r], csem.at[r])
 
+    jload.start()
+    for i in range(parts):
+        pload(i).start()
+    for cp in small:
+        cp.start()
+
+    lax.fori_loop(1, MEM, ring, 0)
+
+    @pl.when(has_up)
+    def _():
+        side(t - 1, 0, 3)
+
+    @pl.when(has_dn)
+    def _():
+        side(t + 1, 3, 0)
+
+    line = jnp.zeros((1, n), f32)
+
+    @pl.when(jnp.logical_not(has_up))
+    def _():
+        for e in range(H):
+            Q[e] = jnp.zeros((G, n), f32)
+            for i in range(3):
+                K[i, e] = line
+        for e in range(2 * H):
+            Rup[e] = line
+
+    @pl.when(jnp.logical_not(has_dn))
+    def _():
+        for e in range(H + rows, E):
+            Q[e] = jnp.zeros((G, n), f32)
+            for i in range(3):
+                K[i, e] = line
+        for e in range(2 * H):
+            Rdn[e] = line
+
+    for cp in small:
+        cp.wait()
+    last = jnp.where(has_dn, 1.0, 0.0).astype(f32)
+    lane = lax.broadcasted_iota(jnp.int32, (1, n), 1)
+    for r in range(rows):
+        row = nat[0, r:r + 1, :]
+        K[0, H + r] = row * last if r == rows - 1 else row
+        K[1, H + r] = jnp.where(lane < n - 1, nat[1, r:r + 1, :], 0.0)
+        K[2, H + r] = nat[2, r:r + 1, :] * natm[r:r + 1, :].astype(f32)
+
+    def qtile(j, carry):
+        cols = pl.ds(pl.multiple_of(j * 128, 128), 128)
+        q = Pv[:, 0, :, cols].astype(f32) * Jv[0, :, cols][None]
+        for v in range(1, 4):
+            q = q + Pv[:, v, :, cols].astype(f32) * Jv[v, :, cols][None]
+        Q[H:H + rows, :, cols] = jnp.swapaxes(q, 0, 1)
+        return carry
+
+    jload.wait()
+    for i in range(parts):
+        pload(i).wait()
+        lax.fori_loop(i * step_cols // 128, (i + 1) * step_cols // 128, qtile, 0)
     for r in range(rows):
         cload(r).start()
+
+    near = jnp.where(z == 0, 16, jnp.where(z == 3, 4, 5))
+    far = jnp.where(z == 3, 16, jnp.where(z == 0, 4, 5))
+    pl.semaphore_wait(bar, MEM - 1 + jnp.where(has_up, near, 0) + jnp.where(has_dn, far, 0))
+
+    def near_copy(src, dst, up, i):
+        return pltpu.make_async_remote_copy(
+            src, dst, hs.at[i], hr.at[i], device_id=(m, t - 1 if up else t + 1), device_id_type=MESH)
+
+    def halo(up):
+        return near_copy(
+            Q.at[pl.ds(H if up else rows, H)], Q.at[pl.ds(H + rows if up else 0, H)], up, 2 if up else 3)
+
+    def piece(up):
+        return near_copy(
+            K.at[:, pl.ds((H if up else rows) + x, 1)], K.at[:, pl.ds((H + rows if up else 0) + x, 1)],
+            up, 0 if up else 1)
+
+    def hand_on(below, i):
+        row = K.at[:, pl.ds((H + rows if below else 0) + x, 1)]
+        k = 0 if below else 1
+        return pltpu.make_async_remote_copy(
+            row, row, fs.at[k], fr.at[k], device_id=(((x + i) % 4) * 4 + z, t), device_id_type=MESH)
+
+    def handed(below):
+        k = 0 if below else 1
+        ref = K.at[:, pl.ds(0, 3)]
+        return pltpu.make_async_remote_copy(
+            ref, ref, fs.at[k], fr.at[k], device_id=(((x + 1) % 4) * 4 + z, t), device_id_type=MESH)
+
+    @pl.when(has_up)
+    def _():
+        piece(True).start()
+
+    @pl.when(has_dn)
+    def _():
+        piece(False).start()
+
+    @pl.when(has_up)
+    def _():
+        halo(True).start()
+
+    @pl.when(has_dn)
+    def _():
+        halo(False).start()
 
     zero = jnp.zeros((G, n), f32)
     for e in list(range(0, H + 1)) + list(range(H + rows + 1, E + 2)):
@@ -89,76 +186,11 @@
     for e in (0, E + 1):
         KR[e] = zero
         KC[e] = zero
-    line = jnp.zeros((1, n), f32)
-
-    @pl.when(jnp.logical_not(has_up))
-    def _():
-        for e in range(H):
-            Q[e] = zero
-            for i in range(3):
-                K[i, e] = line
-        for e in range(2 * H):
-            Rup[e] = line
-
-    @pl.when(jnp.logical_not(has_dn))
-    def _():
-        for e in range(H + rows, E):
-            Q[e] = zero
-            for i in range(3):
-                K[i, e] = line
-        for e in range(2 * H):
-            Rdn[e] = line
-
-    for cp in loads[2:]:
-        cp.wait()
-    last = jnp.where(has_dn, 1.0, 0.0).astype(f32)
-    lane = lax.broadcasted_iota(jnp.int32, (1, n), 1)
-    for r in range(rows):
-        row = nat[0, r:r + 1, :]
-        K[0, H + r] = row * last if r == rows - 1 else row
-        K[1, H + r] = jnp.where(lane < n - 1, nat[1, r:r + 1, :], 0.0)
-        K[2, H + r] = nat[2, r:r + 1, :] * natm[r:r + 1, :].astype(f32)
-
-    loads[0].wait()
-    loads[1].wait()
-
-    def qtile(j, carry):
-        cols = pl.ds(pl.multiple_of(j * 128, 128), 128)
-        q = Pv[:, 0, :, cols].astype(f32) * Jv[0, :, cols][None]
-        for v in range(1, 4):
-            q = q + Pv[:, v, :, cols].astype(f32) * Jv[v, :, cols][None]
-        Q[H:H + rows, :, cols] = jnp.swapaxes(q, 0, 1)
-        return carry
-
-    lax.fori_loop(0, n // 128, qtile, 0)
-
-    near = jnp.where(z == 0, 16, jnp.where(z == 3, 4, 5))
-    far = jnp.where(z == 3, 16, jnp.where(z == 0, 4, 5))
-    pl.semaphore_wait(bar, MEM - 1 + jnp.where(has_up, near, 0) + jnp.where(has_dn, far, 0))
-
-    def halo(buf, up, i):
-        if buf is K:
-            src = K.at[:, pl.ds(H if up else rows, H)]
-            dst = K.at[:, pl.ds(H + rows if up else 0, H)]
-        else:
-            src = Q.at[pl.ds(H if up else rows, H)]
-            dst = Q.at[pl.ds(H + rows if up else 0, H)]
-        return pltpu.make_async_remote_copy(
-            src, dst, hs.at[i], hr.at[i], device_id=(m, t - 1 if up else t + 1), device_id_type=MESH)
-
-    @pl.when(has_up)
-    def _():
-        halo(K, True, 0).start()
-        halo(Q, True, 2).start()
-
-    @pl.when(has_dn)
-    def _():
-        halo(K, False, 1).start()
-        halo(Q, False, 3).start()
-
+        KL[e] = zero
     def widen(e, carry):
         KR[1 + e] = jnp.broadcast_to(K[0, e], (G, n))
         KC[1 + e] = jnp.broadcast_to(K[1, e], (G, n))
+        KL[1 + e] = jnp.broadcast_to(pltpu.roll(K[1, e], 1, 1), (G, n))
         return carry
 
     lax.fori_loop(H, H + rows, widen, 0)
@@ -167,32 +199,52 @@
 
     @pl.when(has_up)
     def _():
-        halo(K, False, 1).wait_recv()
-
-    @pl.when(has_dn)
-    def _():
-        halo(K, True, 0).wait_recv()
+        piece(False).wait_recv()
+        for i in range(1, 4):
+            hand_on(False, i).start()
+
+    @pl.when(has_dn)
+    def _():
+        piece(True).wait_recv()
+        for i in range(1, 4):
+            hand_on(True, i).start()
+
+    @pl.when(has_up)
+    def _():
+        handed(False).wait_recv()
+
+    @pl.when(has_dn)
+    def _():
+        handed(True).wait_recv()
 
     lax.fori_loop(0, H, widen, 0)
     lax.fori_loop(H + rows, E, widen, 0)
 
-    def stencil(src, e):
+    def stencil(src, e, count):
+        outs = []
         v = src[1 + e]
-        down = KR[1 + e] * (src[2 + e] - v)
         up = KR[e] * (v - src[e])
-        flux = KC[1 + e] * (pltpu.roll(v, n - 1, 1) - v)
-        return v + (down - up) + (flux - pltpu.roll(flux, 1, 1))
-
-    def step(src, dst, lo, hi):
-        def body(e, carry):
-            dst[1 + e] = stencil(src, e)
+        for i in range(count):
+            nxt = src[2 + e + i]
+            down = KR[1 + e + i] * (nxt - v)
+            flux = KC[1 + e + i] * (pltpu.roll(v, n - 1, 1) - v)
+            back = KL[1 + e + i] * (v - pltpu.roll(v, 1, 1))
+            outs.append((v + (down - up)) + (flux - back))
+            v, up = nxt, down
+        return outs
+
+    def step(src, dst, lo, hi, group):
+        def body(i, carry):
+            e = lo + i * group
+            for k, o in enumerate(stencil(src, e, group)):
+                dst[1 + e + k] = o
             return carry
-        lax.fori_loop(lo, hi, body, 0)
-
-    step(C, A, H - 1, H + rows + 1)
-    step(A, B, H - 2, H + rows + 2)
-    step(B, A, H - 3, H + rows + 3)
-    step(A, B, 0, E)
+        lax.fori_loop(0, (hi - lo) // group, body, 0)
+
+    step(C, A, H - 1, H + rows + 1, UA)
+    step(A, B, H - 2, H + rows + 2, UB)
+    step(B, A, H - 3, H + rows + 3, UC)
+    step(A, B, 0, E, UD)
 
     def product(e, carry):
         part[e] = jnp.sum(B[1 + e] * Q[e], axis=0, keepdims=True)
@@ -202,11 +254,11 @@
 
     @pl.when(has_up)
     def _():
-        halo(Q, False, 3).wait_recv()
-
-    @pl.when(has_dn)
-    def _():
-        halo(Q, True, 2).wait_recv()
+        halo(False).wait_recv()
+
+    @pl.when(has_dn)
+    def _():
+        halo(True).wait_recv()
 
     lax.fori_loop(0, H, product, 0)
     lax.fori_loop(H + rows, E, product, 0)
@@ -302,30 +354,29 @@
     lax.fori_loop(0, 2 * H, spread_up, 0)
     lax.fori_loop(2 * H, rows, spread_mid, 0)
     lax.fori_loop(rows, E, spread_dn, 0)
-    step(A, B, 1, E - 1)
-    step(B, A, 2, E - 2)
-    step(A, B, 3, E - 3)
+    step(A, B, 1, E - 1, UC)
+    step(B, A, 2, E - 2, UB)
+    step(A, B, 3, E - 3, UA)
 
     def store(r):
         return pltpu.make_async_copy(O.at[r], out.at[:, r, :], osem.at[r])
 
-    def final(r, carry):
-        O[r] = C[1 + H + r] + stencil(B, H + r)
-        return carry
-
-    for r in range(rows):
-        final(r, 0)
-        store(r).start()
-
-    @pl.when(has_up)
-    def _():
-        halo(K, True, 0).wait_send()
-        halo(Q, True, 2).wait_send()
-
-    @pl.when(has_dn)
-    def _():
-        halo(K, False, 1).wait_send()
-        halo(Q, False, 3).wait_send()
+    for r in range(0, rows, UE):
+        for k, o in enumerate(stencil(B, H + r, UE)):
+            O[r + k] = C[1 + H + r + k] + o
+            store(r + k).start()
+
+    @pl.when(has_up)
+    def _():
+        piece(True).wait_send()
+        halo(True).wait_send()
+        handed(False).wait_send()
+
+    @pl.when(has_dn)
+    def _():
+        piece(False).wait_send()
+        halo(False).wait_send()
+        handed(True).wait_send()
 
     for zz in range(4):
         count = owned(zz, 0)[1]
@@ -355,15 +406,15 @@
         in_specs=[pl.BlockSpec(memory_space=pl.ANY)] * 7,
         out_specs=pl.BlockSpec(memory_space=pl.ANY),
         scratch_shapes=[
-            big, big, big, pltpu.VMEM((E, G, n), f32), row(3, E), big, big,
+            big, big, big, pltpu.VMEM((E, G, n), f32), row(3, E), big, big, big,
             pltpu.VMEM(perturbations.shape, jnp.bfloat16), pltpu.VMEM(jacobian.shape, f32),
             pltpu.VMEM((3, rows, n), f32), pltpu.VMEM((rows, n), jnp.int32),
             row(E), row(MEM, 2), row(2), row(E), row(2 * H), row(2 * H),
             pltpu.VMEM((rows, G, n), f32),
-            dma((6,)), dma((rows,)), dma((rows,)), dma((4,)), dma((4,)), dma((4,)), dma((4,)),
+            dma((5,)), dma((n // 256,)), dma((rows,)), dma((rows,)), dma((4,)), dma((4,)), dma((2,)), dma((2,)), dma((4,)), dma((4,)),
         ],
         compiler_params=pltpu.CompilerParams(
-            collective_id=0, has_side_effects=True, vmem_limit_bytes=40 * 1024 * 1024),
+            collective_id=0, has_side_effects=True, vmem_limit_bytes=62 * 1024 * 1024),
     )(controls, perturbations, jacobian, obs_weight, radar_mask, row_faces, col_faces)
 
 

time: 78.5 us -> 52.7 us (0.67)
  the two profiles are of different devices: /device:TPU:24 before, /device:TPU:25 now
where the time goes in v2:
time: 52.7 us; the launch traced here: 52.5 us
  Pallas kernels  50.4 us (96%)
  local copies, waits for them, and re-layouts  2.17 us (4%)
    pallas_call x1, Pallas kernels, per_device(): pl.pallas_call(kernel, out_shape=jax.ShapeDtypeStruct(controls.shape, f32...  50.4 us
    unnamed x1, local copies, waits for them, and re-layouts  2.17 us

profile of v2, /device:TPU:25, one launch (start us, length us, event | category | flops | bytes accessed | tf_op | source)
XLA Modules:
  0.0 52.5 jit_solution(501803865078468834)
XLA Ops:
  0.0 50.4 %shard_map.73 = f32[8,16,1792]{2,1,0:T(8,128)} custom-call(f32[8,16,1792]{2,1,0:T(8,128)} %ctl.1, bf16[8,4,16,1792]{3,2,1,0:T(8,128)(2,1)} %pert.1, f32[4,16,1792]{2,1,0:T(8,128)} %jac.1, f32[16,1792]{1,0:T(8,128)} %obs.1, s32[16,1792]{1,0:T(8,128)} %msk.1, f32[16,1792]{1,0:T(8,128)} %rf.1, f32[16,1792]{1,0:T(8,128)} %cf.1), custom_call_target="tpu_custom_call" | custom-call | tf_op jit(solution)/shard_map/pallas_call | solution.py:403
  50.4 2.2 %copy.9 = f32[8,16,1792]{2,1,0:T(8,128)} copy(f32[8,16,1792]{2,1,0:T(8,128)} %shard_map.73) | data formatting | bytes 1835008

commit v3 on v2

--- a/solution.py
+++ b/solution.py
@@ -141,9 +141,11 @@
         return pltpu.make_async_remote_copy(
             src, dst, hs.at[i], hr.at[i], device_id=(m, t - 1 if up else t + 1), device_id_type=MESH)
 
-    def halo(up):
+    def halo(up, half):
+        k = half * (H // 2)
         return near_copy(
-            Q.at[pl.ds(H if up else rows, H)], Q.at[pl.ds(H + rows if up else 0, H)], up, 2 if up else 3)
+            Q.at[pl.ds((H if up else rows) + k, H // 2)], Q.at[pl.ds((H + rows if up else 0) + k, H // 2)],
+            up, (2 if up else 4) + half)
 
     def piece(up):
         return near_copy(
@@ -170,13 +172,16 @@
     def _():
         piece(False).start()
 
-    @pl.when(has_up)
-    def _():
-        halo(True).start()
-
-    @pl.when(has_dn)
-    def _():
-        halo(False).start()
+    def send_half(half):
+        @pl.when(has_up)
+        def _():
+            halo(True, half).start()
+
+        @pl.when(has_dn)
+        def _():
+            halo(False, half).start()
+
+    send_half(0)
 
     zero = jnp.zeros((G, n), f32)
     for e in list(range(0, H + 1)) + list(range(H + rows + 1, E + 2)):
@@ -209,6 +214,8 @@
         for i in range(1, 4):
             hand_on(True, i).start()
 
+    send_half(1)
+
     @pl.when(has_up)
     def _():
         handed(False).wait_recv()
@@ -252,86 +259,88 @@
 
     lax.fori_loop(H, H + rows, product, 0)
 
-    @pl.when(has_up)
-    def _():
-        halo(False).wait_recv()
-
-    @pl.when(has_dn)
-    def _():
-        halo(True).wait_recv()
+    peer = (m + 1) % MEM
+
+    def to(src, dst, sem, mm, tt):
+        return pltpu.make_async_remote_copy(
+            src, dst, ss.at[sem], sr.at[sem], device_id=(mm, tt), device_id_type=MESH)
+
+    def waiter(ref, sem):
+        return to(ref, ref, sem, peer, t)
+
+    mine = H + 4 * z + x
+    late = jnp.where(z == 0, x, H + rows + x)
+    owner_late = jnp.logical_or(z == 0, z == 3)
+
+    def scatter(i, carry):
+        o = (m + i) % MEM
+        to(part.at[pl.ds(H + 4 * (o % 4) + o // 4, 1)], recv.at[0, pl.ds(m, 1)], 0, o, t).start()
+        return carry
+
+    lax.fori_loop(1, MEM, scatter, 0)
+
+    @pl.when(has_up)
+    def _():
+        halo(False, 0).wait_recv()
+        halo(False, 1).wait_recv()
+
+    @pl.when(has_dn)
+    def _():
+        halo(True, 0).wait_recv()
+        halo(True, 1).wait_recv()
 
     lax.fori_loop(0, H, product, 0)
     lax.fori_loop(H + rows, E, product, 0)
 
-    def owned(zz, xx):
-        return ((2 * xx, 2), (8 + xx, 1), (12 + xx, 1), (16 + 2 * xx, 2))[zz]
-
-    def scatter(i, carry):
-        xx = (x + i) % 4
-        for zz in range(4):
-            start, count = owned(zz, xx)
-
+    def scatter_late(i, carry):
+        xx = (x + 3 - i) % 4
+        for zz, start in ((0, 0), (3, H + rows)):
             @pl.when(jnp.logical_or(xx != x, z != zz))
             def _():
-                pltpu.make_async_remote_copy(
-                    part.at[pl.ds(start, count)], recv.at[m, pl.ds(0, count)], ss.at[0], sr.at[0],
-                    device_id=(xx * 4 + zz, t), device_id_type=MESH).start()
-        return carry
-
-    lax.fori_loop(0, 4, scatter, 0)
-
-    peer = (m + 1) % MEM
-
-    def waiter(ref, sems):
-        return pltpu.make_async_remote_copy(ref, ref, sems[0], sems[1], device_id=(peer, t), device_id_type=MESH)
-
-    rs = (ss.at[0], sr.at[0])
-    ag = (ss.at[1], sr.at[1])
-    nu = (ss.at[2], sr.at[2])
-    nd = (ss.at[3], sr.at[3])
-    for zz in range(4):
-        start, count = owned(zz, x)
-
-        @pl.when(z == zz)
-        def _():
-            recv[m, 0:count] = part[pl.ds(start, count)]
-            waiter(recv.at[pl.ds(0, MEM - 1), pl.ds(0, count)], rs).wait_recv()
-            total = recv[0, 0:count]
-            for i in range(1, MEM):
-                total = total + recv[i, 0:count]
-            rown[0:count] = total
-            R[pl.ds(start, count)] = total
-
-            def gather(i, carry):
-                pltpu.make_async_remote_copy(
-                    rown.at[pl.ds(0, count)], R.at[pl.ds(start, count)], ag[0], ag[1],
-                    device_id=((m + i) % MEM, t), device_id_type=MESH).start()
-                return carry
-
-            if zz in (0, 3):
-                near = has_up if zz == 0 else has_dn
-                sem = nu if zz == 0 else nd
-                dst = Rdn if zz == 0 else Rup
-
-                @pl.when(near)
-                def _():
-                    def cross(i, carry):
-                        pltpu.make_async_remote_copy(
-                            rown.at[pl.ds(0, 2)], dst.at[pl.ds(2 * x, 2)], sem[0], sem[1],
-                            device_id=((m + i) % MEM, t - 1 if zz == 0 else t + 1), device_id_type=MESH).start()
-                        return carry
-                    lax.fori_loop(0, MEM, cross, 0)
-
-            lax.fori_loop(1, MEM, gather, 0)
-            waiter(R.at[pl.ds(0, E - count)], ag).wait_recv()
-
-    @pl.when(has_up)
-    def _():
-        waiter(Rup, nd).wait_recv()
-
-    @pl.when(has_dn)
-    def _():
-        waiter(Rdn, nu).wait_recv()
+                to(part.at[pl.ds(start + xx, 1)], recv.at[1, pl.ds(m, 1)], 1, xx * 4 + zz, t).start()
+        return carry
+
+    lax.fori_loop(0, 4, scatter_late, 0)
+
+    def total(k, row):
+        recv[k, pl.ds(m, 1)] = part[pl.ds(row, 1)]
+        waiter(recv.at[k, pl.ds(0, MEM - 1)], k).wait_recv()
+        sums = [recv[k, i:i + 1] for i in range(MEM)]
+        while len(sums) > 1:
+            sums = [a + b for a, b in zip(sums[::2], sums[1::2])]
+        rown[k:k + 1] = sums[0]
+        R[pl.ds(row, 1)] = sums[0]
+
+    def gather(k, row):
+        src = rown.at[pl.ds(k, 1)]
+
+        def cross(i, carry, dst, at, sem, tt):
+            to(src, dst.at[pl.ds(at, 1)], sem, (m + i) % MEM, tt).start()
+            return carry
+
+        @pl.when(jnp.logical_and(z == 0, has_up))
+        def _():
+            lax.fori_loop(0, MEM, lambda i, c: cross(i, c, Rdn, row, 4 + k, t - 1), 0)
+
+        @pl.when(jnp.logical_and(z == 3, has_dn))
+        def _():
+            lax.fori_loop(0, MEM, lambda i, c: cross(i, c, Rup, row - rows, 6 + k, t + 1), 0)
+
+        def own(i, carry):
+            to(src, R.at[pl.ds(row, 1)], 2 + k, (m + i) % MEM, t).start()
+            return carry
+
+        lax.fori_loop(1, MEM, own, 0)
+
+    total(0, mine)
+    gather(0, mine)
+
+    @pl.when(owner_late)
+    def _():
+        total(1, late)
+        gather(1, late)
+
+    waiter(R.at[pl.ds(0, MEM - 1)], 2).wait_recv()
 
     def spread(e, extra):
         r = R[e]
@@ -351,8 +360,33 @@
         spread(e, Rdn[e - rows])
         return carry
 
+    lax.fori_loop(2 * H, rows, spread_mid, 0)
+
+    @pl.when(has_up)
+    def _():
+        waiter(Rup.at[pl.ds(0, H)], 6).wait_recv()
+
+    @pl.when(has_dn)
+    def _():
+        waiter(Rdn.at[pl.ds(0, H)], 4).wait_recv()
+
+    @pl.when(owner_late)
+    def _():
+        waiter(R.at[pl.ds(0, 2 * H - 1)], 3).wait_recv()
+
+    @pl.when(jnp.logical_not(owner_late))
+    def _():
+        waiter(R.at[pl.ds(0, 2 * H)], 3).wait_recv()
+
+    @pl.when(has_up)
+    def _():
+        waiter(Rup.at[pl.ds(0, H)], 7).wait_recv()
+
+    @pl.when(has_dn)
+    def _():
+        waiter(Rdn.at[pl.ds(0, H)], 5).wait_recv()
+
     lax.fori_loop(0, 2 * H, spread_up, 0)
-    lax.fori_loop(2 * H, rows, spread_mid, 0)
     lax.fori_loop(rows, E, spread_dn, 0)
     step(A, B, 1, E - 1, UC)
     step(B, A, 2, E - 2, UB)
@@ -369,26 +403,34 @@
     @pl.when(has_up)
     def _():
         piece(True).wait_send()
-        halo(True).wait_send()
+        halo(True, 0).wait_send()
+        halo(True, 1).wait_send()
         handed(False).wait_send()
 
     @pl.when(has_dn)
     def _():
         piece(False).wait_send()
-        halo(False).wait_send()
+        halo(False, 0).wait_send()
+        halo(False, 1).wait_send()
         handed(True).wait_send()
 
-    for zz in range(4):
-        count = owned(zz, 0)[1]
-
-        @pl.when(z == zz)
-        def _():
-            waiter(part.at[pl.ds(0, E - count)], rs).wait_send()
-            waiter(recv.at[pl.ds(0, MEM - 1), pl.ds(0, count)], ag).wait_send()
-            if zz in (0, 3):
-                @pl.when(has_up if zz == 0 else has_dn)
-                def _():
-                    waiter(recv, nu if zz == 0 else nd).wait_send()
+    waiter(R.at[pl.ds(0, MEM - 1)], 0).wait_send()
+    waiter(R.at[pl.ds(0, MEM - 1)], 2).wait_send()
+
+    @pl.when(owner_late)
+    def _():
+        waiter(R.at[pl.ds(0, 2 * H - 1)], 1).wait_send()
+        waiter(R.at[pl.ds(0, MEM - 1)], 3).wait_send()
+
+    @pl.when(jnp.logical_not(owner_late))
+    def _():
+        waiter(R.at[pl.ds(0, 2 * H)], 1).wait_send()
+
+    for zz, near, k in ((0, has_up, 4), (3, has_dn, 6)):
+        @pl.when(jnp.logical_and(z == zz, near))
+        def _():
+            waiter(R.at[pl.ds(0, MEM)], k).wait_send()
+            waiter(R.at[pl.ds(0, MEM)], k + 1).wait_send()
 
     for r in range(rows):
         store(r).wait()
@@ -409,9 +451,9 @@
             big, big, big, pltpu.VMEM((E, G, n), f32), row(3, E), big, big, big,
             pltpu.VMEM(perturbations.shape, jnp.bfloat16), pltpu.VMEM(jacobian.shape, f32),
             pltpu.VMEM((3, rows, n), f32), pltpu.VMEM((rows, n), jnp.int32),
-            row(E), row(MEM, 2), row(2), row(E), row(2 * H), row(2 * H),
+            row(E), row(2, MEM), row(2), row(E), row(2 * H), row(2 * H),
             pltpu.VMEM((rows, G, n), f32),
-            dma((5,)), dma((n // 256,)), dma((rows,)), dma((rows,)), dma((4,)), dma((4,)), dma((2,)), dma((2,)), dma((4,)), dma((4,)),
+            dma((5,)), dma((n // 256,)), dma((rows,)), dma((rows,)), dma((6,)), dma((6,)), dma((2,)), dma((2,)), dma((8,)), dma((8,)),
         ],
         compiler_params=pltpu.CompilerParams(
             collective_id=0, has_side_effects=True, vmem_limit_bytes=62 * 1024 * 1024),

time: 52.7 us -> 51.1 us (0.970)
  the two profiles are of different devices: /device:TPU:25 before, /device:TPU:16 now
where the time goes in v3:
time: 51.1 us; the launch traced here: 50.9 us
  Pallas kernels  48.7 us (95%)
  local copies, waits for them, and re-layouts  2.17 us (4%)
    pallas_call x1, Pallas kernels, per_device(): pl.pallas_call(kernel, out_shape=jax.ShapeDtypeStruct(controls.shape, f32...  48.7 us
    unnamed x1, local copies, waits for them, and re-layouts  2.17 us

profile of v3, /device:TPU:16, one launch (start us, length us, event | category | flops | bytes accessed | tf_op | source)
XLA Modules:
  0.0 50.9 jit_solution(1983930377637700064)
XLA Ops:
  0.0 48.7 %shard_map.73 = f32[8,16,1792]{2,1,0:T(8,128)} custom-call(f32[8,16,1792]{2,1,0:T(8,128)} %ctl.1, bf16[8,4,16,1792]{3,2,1,0:T(8,128)(2,1)} %pert.1, f32[4,16,1792]{2,1,0:T(8,128)} %jac.1, f32[16,1792]{1,0:T(8,128)} %obs.1, s32[16,1792]{1,0:T(8,128)} %msk.1, f32[16,1792]{1,0:T(8,128)} %rf.1, f32[16,1792]{1,0:T(8,128)} %cf.1), custom_call_target="tpu_custom_call" | custom-call | tf_op jit(solution)/shard_map/pallas_call | solution.py:445
  48.7 2.2 %copy.9 = f32[8,16,1792]{2,1,0:T(8,128)} copy(f32[8,16,1792]{2,1,0:T(8,128)} %shard_map.73) | data formatting | bytes 1835008

commit v4 on v3

--- a/solution.py
+++ b/solution.py
@@ -10,11 +10,11 @@
 H = 4
 MESH = pl.DeviceIdType.MESH
 f32 = jnp.float32
-UA, UB, UC, UD, UE = 9, 5, 11, 8, 8
+UE = 8
 
 
 def kernel(ctl, pert, jac, obs, msk, rf, cf, out,
-           C, A, B, Q, K, KR, KC, KL, Pv, Jv, nat, natm, part, recv, rown, R, Rup, Rdn, O,
+           C, A, B, A2, B2, Q, K, KR, KC, KL, Pv, Jv, nat, natm, part, recv, rown, R, Rup, Rdn, O,
            lsem, psem, csem, osem, hs, hr, fs, fr, ss, sr):
     G = Q.shape[1]
     n = Q.shape[2]
@@ -80,13 +80,13 @@
 
     lax.fori_loop(1, MEM, ring, 0)
 
+    @pl.when(has_dn)
+    def _():
+        side(t + 1, 3, 0)
+
     @pl.when(has_up)
     def _():
         side(t - 1, 0, 3)
-
-    @pl.when(has_dn)
-    def _():
-        side(t + 1, 3, 0)
 
     line = jnp.zeros((1, n), f32)
 
@@ -188,6 +188,8 @@
         C[e] = zero
         A[e] = zero
         B[e] = zero
+        A2[e] = zero
+        B2[e] = zero
     for e in (0, E + 1):
         KR[e] = zero
         KC[e] = zero
@@ -199,34 +201,6 @@
         return carry
 
     lax.fori_loop(H, H + rows, widen, 0)
-    for r in range(rows):
-        cload(r).wait()
-
-    @pl.when(has_up)
-    def _():
-        piece(False).wait_recv()
-        for i in range(1, 4):
-            hand_on(False, i).start()
-
-    @pl.when(has_dn)
-    def _():
-        piece(True).wait_recv()
-        for i in range(1, 4):
-            hand_on(True, i).start()
-
-    send_half(1)
-
-    @pl.when(has_up)
-    def _():
-        handed(False).wait_recv()
-
-    @pl.when(has_dn)
-    def _():
-        handed(True).wait_recv()
-
-    lax.fori_loop(0, H, widen, 0)
-    lax.fori_loop(H + rows, E, widen, 0)
-
     def stencil(src, e, count):
         outs = []
         v = src[1 + e]
@@ -248,13 +222,51 @@
             return carry
         lax.fori_loop(0, (hi - lo) // group, body, 0)
 
-    step(C, A, H - 1, H + rows + 1, UA)
-    step(A, B, H - 2, H + rows + 2, UB)
-    step(B, A, H - 3, H + rows + 3, UC)
-    step(A, B, 0, E, UD)
+    for r in range(rows):
+        cload(r).wait()
+
+    step(C, A, H + 1, H + rows - 1, 7)
+    step(A, B, H + 2, H + rows - 2, 6)
+    step(B, A2, H + 3, H + rows - 3, 10)
+    step(A2, B2, H + 4, H + rows - 4, 8)
+
+    @pl.when(has_up)
+    def _():
+        piece(False).wait_recv()
+        for i in range(1, 4):
+            hand_on(False, i).start()
+
+    @pl.when(has_dn)
+    def _():
+        piece(True).wait_recv()
+        for i in range(1, 4):
+            hand_on(True, i).start()
+
+    send_half(1)
+
+    @pl.when(has_up)
+    def _():
+        handed(False).wait_recv()
+
+    @pl.when(has_dn)
+    def _():
+        handed(True).wait_recv()
+
+    lax.fori_loop(0, H, widen, 0)
+    lax.fori_loop(H + rows, E, widen, 0)
+
+    def edges(src, dst, width):
+        for lo in (H - width, H + rows - width):
+            for k, o in enumerate(stencil(src, lo, 2 * width)):
+                dst[1 + lo + k] = o
+
+    edges(C, A, 1)
+    edges(A, B, 2)
+    edges(B, A2, 3)
+    edges(A2, B2, 4)
 
     def product(e, carry):
-        part[e] = jnp.sum(B[1 + e] * Q[e], axis=0, keepdims=True)
+        part[e] = jnp.sum(B2[1 + e] * Q[e], axis=0, keepdims=True)
         return carry
 
     lax.fori_loop(H, H + rows, product, 0)
@@ -361,6 +373,9 @@
         return carry
 
     lax.fori_loop(2 * H, rows, spread_mid, 0)
+    step(A, B, 2 * H + 1, rows - 1, 6)
+    step(B, A2, 2 * H + 2, rows - 2, 4)
+    step(A2, B2, 2 * H + 3, rows - 3, 2)
 
     @pl.when(has_up)
     def _():
@@ -388,15 +403,20 @@
 
     lax.fori_loop(0, 2 * H, spread_up, 0)
     lax.fori_loop(rows, E, spread_dn, 0)
-    step(A, B, 1, E - 1, UC)
-    step(B, A, 2, E - 2, UB)
-    step(A, B, 3, E - 3, UA)
+    def rims(src, dst, s):
+        for lo in (s, rows - s):
+            for k, o in enumerate(stencil(src, lo, 2 * H)):
+                dst[1 + lo + k] = o
+
+    rims(A, B, 1)
+    rims(B, A2, 2)
+    rims(A2, B2, 3)
 
     def store(r):
         return pltpu.make_async_copy(O.at[r], out.at[:, r, :], osem.at[r])
 
     for r in range(0, rows, UE):
-        for k, o in enumerate(stencil(B, H + r, UE)):
+        for k, o in enumerate(stencil(B2, H + r, UE)):
             O[r + k] = C[1 + H + r + k] + o
             store(r + k).start()
 
@@ -448,7 +468,7 @@
         in_specs=[pl.BlockSpec(memory_space=pl.ANY)] * 7,
         out_specs=pl.BlockSpec(memory_space=pl.ANY),
         scratch_shapes=[
-            big, big, big, pltpu.VMEM((E, G, n), f32), row(3, E), big, big, big,
+            big, big, big, big, big, pltpu.VMEM((E, G, n), f32), row(3, E), big, big, big,
             pltpu.VMEM(perturbations.shape, jnp.bfloat16), pltpu.VMEM(jacobian.shape, f32),
             pltpu.VMEM((3, rows, n), f32), pltpu.VMEM((rows, n), jnp.int32),
             row(E), row(2, MEM), row(2), row(E), row(2 * H), row(2 * H),

time: 51.1 us -> 49.1 us (0.961)
  Pallas kernels: 48.7 us -> 46.7 us
    pallas_call x1, Pallas kernels: 48.7 us -> 46.7 us  [per_device(): pl.pallas_call(kernel, out_shape=jax.ShapeDtypeStruct(controls.shape, f32...]
where the time goes in v4:
time: 49.1 us; the launch traced here: 48.9 us
  Pallas kernels  46.7 us (95%)
  local copies, waits for them, and re-layouts  2.17 us (4%)
    pallas_call x1, Pallas kernels, per_device(): pl.pallas_call(kernel, out_shape=jax.ShapeDtypeStruct(controls.shape, f32...  46.7 us
    unnamed x1, local copies, waits for them, and re-layouts  2.17 us

profile of v4, /device:TPU:16, one launch (start us, length us, event | category | flops | bytes accessed | tf_op | source)
XLA Modules:
  0.0 48.9 jit_solution(17829772132769730447)
XLA Ops:
  0.0 46.7 %shard_map.73 = f32[8,16,1792]{2,1,0:T(8,128)} custom-call(f32[8,16,1792]{2,1,0:T(8,128)} %ctl.1, bf16[8,4,16,1792]{3,2,1,0:T(8,128)(2,1)} %pert.1, f32[4,16,1792]{2,1,0:T(8,128)} %jac.1, f32[16,1792]{1,0:T(8,128)} %obs.1, s32[16,1792]{1,0:T(8,128)} %msk.1, f32[16,1792]{1,0:T(8,128)} %rf.1, f32[16,1792]{1,0:T(8,128)} %cf.1), custom_call_target="tpu_custom_call" | custom-call | tf_op jit(solution)/shard_map/pallas_call | solution.py:465
  46.8 2.2 %copy.9 = f32[8,16,1792]{2,1,0:T(8,128)} copy(f32[8,16,1792]{2,1,0:T(8,128)} %shard_map.73) | data formatting | bytes 1835008

commit v5 on v4

--- a/solution.py
+++ b/solution.py
@@ -22,8 +22,8 @@
     rows = E - 2 * H
     m = lax.axis_index("mem")
     t = lax.axis_index("tile")
-    x = m // 4
-    z = m % 4
+    x = lax.div(m, 4)
+    z = lax.rem(m, 4)
     has_up = t > 0
     has_dn = t < TILE - 1
 
@@ -33,7 +33,7 @@
         pl.semaphore_signal(bar, inc=1, device_id=(mm, tt), device_id_type=MESH)
 
     def ring(i, carry):
-        greet((m + i) % MEM, t)
+        greet(lax.rem(m + i, MEM), t)
         return carry
 
     def side(tt, full_z, own_z):
@@ -156,7 +156,7 @@
         row = K.at[:, pl.ds((H + rows if below else 0) + x, 1)]
         k = 0 if below else 1
         return pltpu.make_async_remote_copy(
-            row, row, fs.at[k], fr.at[k], device_id=(((x + i) % 4) * 4 + z, t), device_id_type=MESH)
+            row, row, fs.at[k], fr.at[k], device_id=(lax.rem(x + i, 4) * 4 + z, t), device_id_type=MESH)
 
     def handed(below):
         k = 0 if below else 1
@@ -285,8 +285,8 @@
     owner_late = jnp.logical_or(z == 0, z == 3)
 
     def scatter(i, carry):
-        o = (m + i) % MEM
-        to(part.at[pl.ds(H + 4 * (o % 4) + o // 4, 1)], recv.at[0, pl.ds(m, 1)], 0, o, t).start()
+        o = lax.rem(m + i, MEM)
+        to(part.at[pl.ds(H + 4 * lax.rem(o, 4) + lax.div(o, 4), 1)], recv.at[0, pl.ds(m, 1)], 0, o, t).start()
         return carry
 
     lax.fori_loop(1, MEM, scatter, 0)
@@ -305,7 +305,7 @@
     lax.fori_loop(H + rows, E, product, 0)
 
     def scatter_late(i, carry):
-        xx = (x + 3 - i) % 4
+        xx = lax.rem(x + 3 - i + 4, 4)
         for zz, start in ((0, 0), (3, H + rows)):
             @pl.when(jnp.logical_or(xx != x, z != zz))
             def _():
@@ -327,7 +327,7 @@
         src = rown.at[pl.ds(k, 1)]
 
         def cross(i, carry, dst, at, sem, tt):
-            to(src, dst.at[pl.ds(at, 1)], sem, (m + i) % MEM, tt).start()
+            to(src, dst.at[pl.ds(at, 1)], sem, lax.rem(m + i, MEM), tt).start()
             return carry
 
         @pl.when(jnp.logical_and(z == 0, has_up))
@@ -339,7 +339,7 @@
             lax.fori_loop(0, MEM, lambda i, c: cross(i, c, Rup, row - rows, 6 + k, t + 1), 0)
 
         def own(i, carry):
-            to(src, R.at[pl.ds(row, 1)], 2 + k, (m + i) % MEM, t).start()
+            to(src, R.at[pl.ds(row, 1)], 2 + k, lax.rem(m + i, MEM), t).start()
             return carry
 
         lax.fori_loop(1, MEM, own, 0)

time: 49.1 us -> 49.1 us (level)
  no operation moved by 1% of the time
where the time goes in v5:
time: 49.1 us; the launch traced here: 48.9 us
  Pallas kernels  46.7 us (95%)
  local copies, waits for them, and re-layouts  2.17 us (4%)
    pallas_call x1, Pallas kernels, per_device(): pl.pallas_call(kernel, out_shape=jax.ShapeDtypeStruct(controls.shape, f32...  46.7 us
    unnamed x1, local copies, waits for them, and re-layouts  2.17 us

profile of v5, /device:TPU:16, one launch (start us, length us, event | category | flops | bytes accessed | tf_op | source)
XLA Modules:
  0.0 48.9 jit_solution(14756265089179871134)
XLA Ops:
  0.0 46.7 %shard_map.73 = f32[8,16,1792]{2,1,0:T(8,128)} custom-call(f32[8,16,1792]{2,1,0:T(8,128)} %ctl.1, bf16[8,4,16,1792]{3,2,1,0:T(8,128)(2,1)} %pert.1, f32[4,16,1792]{2,1,0:T(8,128)} %jac.1, f32[16,1792]{1,0:T(8,128)} %obs.1, s32[16,1792]{1,0:T(8,128)} %msk.1, f32[16,1792]{1,0:T(8,128)} %rf.1, f32[16,1792]{1,0:T(8,128)} %cf.1), custom_call_target="tpu_custom_call" | custom-call | tf_op jit(solution)/shard_map/pallas_call | solution.py:465
  46.7 2.2 %copy.9 = f32[8,16,1792]{2,1,0:T(8,128)} copy(f32[8,16,1792]{2,1,0:T(8,128)} %shard_map.73) | data formatting | bytes 1835008
